TPU v7x, 32 devices: a whole 2x2x4 slice. The times are simulated.
32 devices in a mesh: ctx: 2 (over core), row: 4 (over y, x), col: 4 (over z).
Axes of the slice: x: 2, y: 2, z: 4, core: 2. Of those that a mesh axis runs over, the one named last changes fastest.
Arguments:
- output_grad: bfloat16 [1024, 8192], P('ctx', ('row', 'col')), may hold values from -6 to 6
- conv_out: bfloat16 [1024, 8192], P('ctx', ('row', 'col')), may hold values from -9 to 9
- input_mix: bfloat16 [1024, 4, 256], P('ctx'), may hold values from -0.5 to 0.5
- output_mix: bfloat16 [1024, 4, 256], P('ctx'), may hold values from -1 to 1
- step_size: float32 [128, 1024], P(('row', 'col'), 'ctx'), may hold values from 0.5 to 2
- log_decay: float32 [128, 1024], P(('row', 'col'), 'ctx'), may hold values from -2.1 to 0, as said below
- skip_gain: float32 [128], P(('row', 'col')), may hold values from 0.5 to 2
- conv_weight: float32 [4, 8192], P(None, ('row', 'col')), may hold values from -3 to 3
- later_grad: float32 [128, 64, 256], P(('row', 'col')), may hold values from -6 to 6
- proj_weight: bfloat16 [8192, 8192], P('col', 'row'), may hold values from -0.0625 to 0.0625
Outputs:
- hidden_grad: bfloat16 [1024, 8192], P('ctx', ('col', 'row'))
- x_grad: bfloat16 [1024, 8192], P('ctx', ('row', 'col'))
- state_grad: float32 [2, 128, 64, 256], P('ctx', ('row', 'col'))
Inputs may be any that keep to these rules, and one draw needn't show every extreme that they name: `log_decay`: the forward pass's log decay of each head at each token.
All inputs are finite; a program needn't handle non-finite values.
Results may differ from a plain program's by a relative error of at most 0.022.
Values may be sent and summed in bfloat16 or wider, within the bound.
A program may use at most 128 MiB of HBM per device.

v0:
```python
import jax
import jax.numpy as jnp
from jax import lax
from jax.sharding import PartitionSpec as P

HD = 64
HPG = 32
KW = 4


def from_behind(value, axis, steps):
    count = lax.axis_size(axis)
    first, last = (max(0, -steps), min(count, count - steps))
    return lax.ppermute(value, axis, [(source, source + steps) for source in range(first, last)])


def on_device(
    output_grad,
    conv_out,
    input_mix,
    output_mix,
    step_size,
    log_decay,
    skip_gain,
    conv_weight,
    later_grad,
    proj_weight,
):
    tokens_dev = output_grad.shape[0]
    heads_dev = step_size.shape[0]
    head_block = lax.axis_index("row") * lax.axis_size("col") + lax.axis_index("col")
    group = head_block * heads_dev // HPG
    write_rows = lax.dynamic_index_in_dim(input_mix, group, 1, keepdims=False)
    read_rows = lax.dynamic_index_in_dim(output_mix, group, 1, keepdims=False)
    cumulative = jnp.cumsum(log_decay, axis=1)
    block_end = cumulative[:, -1]
    decays = jnp.exp(block_end)
    per_head = output_grad.reshape(tokens_dev, heads_dev, HD)
    weighted = (jnp.exp(cumulative).T[:, :, None] * per_head.astype(jnp.float32)).astype(
        jnp.bfloat16
    )
    block_sum = jnp.einsum("shd,sn->hdn", weighted, read_rows, preferred_element_type=jnp.float32)
    is_last = lax.axis_index("ctx") == lax.axis_size("ctx") - 1

    def chain_turn(turn_index, estimate):
        passed = from_behind(
            (block_sum + decays[:, None, None] * estimate).astype(jnp.bfloat16), "ctx", -1
        ).astype(jnp.float32)
        return jnp.where(is_last, later_grad, passed)

    carried = lax.fori_loop(
        0,
        lax.axis_size("ctx") - 1,
        chain_turn,
        jnp.where(is_last, later_grad, jnp.zeros_like(later_grad)),
    )
    state_start = block_sum + decays[:, None, None] * carried
    scores = jnp.dot(write_rows, read_rows.T, preferred_element_type=jnp.float32)
    positions = jnp.arange(tokens_dev)
    causal = positions[None, :] >= positions[:, None]
    offsets = cumulative[:, None, :] - cumulative[:, :, None]
    mixing = (jnp.exp(jnp.where(causal[None], offsets, -jnp.inf)) * scores[None]).astype(
        jnp.bfloat16
    )
    intra = jnp.einsum("hts,shd->thd", mixing, per_head, preferred_element_type=jnp.float32)
    inter = jnp.einsum(
        "hdn,tn->thd", carried, write_rows.astype(jnp.float32), precision=lax.Precision.HIGHEST
    )
    inter = inter * jnp.exp(block_end[:, None] - cumulative).T[:, :, None]
    input_grad = step_size.T[:, :, None] * (intra + inter) + skip_gain[
        None, :, None
    ] * per_head.astype(jnp.float32)
    flat_grad = input_grad.reshape(tokens_dev, heads_dev * HD)
    activated = conv_out.astype(jnp.float32)
    sigma = jax.nn.sigmoid(activated)
    pre_grad = (flat_grad * sigma * (1.0 + activated * (1.0 - sigma))).astype(jnp.bfloat16)
    rim_rows = from_behind(pre_grad[: KW - 1], "ctx", -1)
    extended = jnp.concatenate([pre_grad, rim_rows], axis=0).astype(jnp.float32)
    accum = jnp.zeros(pre_grad.shape, jnp.float32)
    for tap in range(KW):
        accum = accum + conv_weight[tap][None, :] * extended[tap : tap + tokens_dev]
    x_grad = accum.astype(jnp.bfloat16)
    partial_grad = lax.dot_general(
        lax.all_gather(x_grad, "col", axis=1, tiled=True),
        proj_weight,
        (((1,), (1,)), ((), ())),
        preferred_element_type=jnp.float32,
    )
    hidden_grad = lax.psum_scatter(
        partial_grad.astype(jnp.bfloat16), "row", scatter_dimension=1, tiled=True
    )
    return (hidden_grad, x_grad, state_start[None])


def solution(mesh):
    return jax.shard_map(
        on_device,
        mesh=mesh,
        in_specs=(
            P("ctx", ("row", "col")),
            P("ctx", ("row", "col")),
            P("ctx", None, None),
            P("ctx", None, None),
            P(("row", "col"), "ctx"),
            P(("row", "col"), "ctx"),
            P(("row", "col")),
            P(None, ("row", "col")),
            P(("row", "col"), None, None),
            P("col", "row"),
        ),
        out_specs=(
            P("ctx", ("col", "row")),
            P("ctx", ("row", "col")),
            P("ctx", ("row", "col"), None, None),
        ),
        check_vma=False,
    )
```

profile of v0, /device:TPU:0, one launch (start us, length us, event | category | flops | bytes accessed | tf_op | source)
XLA Modules:
  0.0 126.2 jit_solution(12373785382565154950)
XLA Ops:
  7.2 2.3 %reduce-window.6 = f32[8,4,128]{2,0,1:T(8,128)S(1)} reduce-window(f32[8,4,128]{2,0,1:T(8,128)} %bitcast.47, f32[]{:T(128)} %constant.39.clone.1), window={size=1x1x128 pad=0_0x0_0x127_0}, to_apply=%region_0.1 | reduce-window | flops 520192 | bytes 32772 | tf_op jit(solution)/shard_map/reduce-window
  9.5 0.2 slice_reduce_fusion
  9.7 0.1 exponential_bitcast_fusion.1
  9.8 0.2 slice_reduce_fusion.1
  10.0 1.3 %copy.26 = bf16[512,512]{0,1:T(8,128)(2,1)S(1)} copy(bf16[512,512]{1,0:T(8,128)(2,1)} %param.10) | data formatting | bytes 1048576 | tf_op args[0]
  11.3 0.1 fusion.16
  11.4 0.5 constant_dynamic-slice_fusion
  12.0 0.3 add_convert_fusion
  12.3 1.3 %collective-permute-start = (bf16[8,64,256]{2,1,0:T(8,128)(2,1)S(1)}, bf16[8,64,256]{2,1,0:T(8,128)(2,1)S(1)}, u32[]{:S(2)}, u32[]{:S(2)}) collective-permute-start(bf16[8,64,256]{2,1,0:T(8,128)(2,1)S(1)} %get-tuple-element.27), channel_id=1, source_target_pairs={{16,0},{17,1},{18,2},{19,3},{20,4},{21,5},{22,6},{23,7},{24,8},{25... | collective-permute-start | bytes 786440 | tf_op jit(solution)/shard_map/while/body/eval_jaxpr/ppermute | solution.py:14
  13.6 0.1 iota_compare_fusion
  13.7 0.5 constant_dynamic-slice_fusion.1
  14.2 0.3 fusion.20
  14.6 2.6 %fusion.2 = f32[512,8,64]{0,2,1:T(8,128)S(1)} fusion(bf16[512,8,64]{0,2,1:T(8,128)(2,1)S(1)} %bitcast.42, f32[512,512]{1,0:T(8,128)S(1)} %fusion.20, f32[8,512]{1,0:T(8,128)S(1)} %get-tuple-element.16, pred[512,512]{1,0:T(8,128)(4,1)S(1)} %iota_compare_fusion), kind=kOutput, calls=%fused_computation.4 | convolution fusion | flops 276824064 | bytes 2899968 | tf_op jit(solution)/shard_map/hts,shd->thd/dot_general | solution.py:65
  17.3 1.8 %fusion.5 = f32[512,8,64]{0,2,1:T(8,128)} fusion(f32[512,8,64]{0,2,1:T(8,128)S(1)} %fusion.2, bf16[512,8,64]{0,2,1:T(8,128)(2,1)S(1)} %bitcast.43, f32[8]{0:T(128)S(1)} %copy-done.5, f32[512,8]{0,1:T(8,128)S(1)} %exponential_bitcast_fusion, f32[512,8]{0,1:T(8,128)S(1)} %bitcast.46, f32[8,64,256]{2,1,0:T(8,128)S(1)} %copy-done.1, ...), kind=kOutput, calls=%fused_computation.8 | convolution fusion | flops 807141376 | bytes 3702817 | tf_op jit(solution)/shard_map/hdn,tn->thd/dot_general | solution.py:66
  19.1 1.6 %copy.28 = f32[512,512]{1,0:T(8,128)S(1)} copy(f32[512,512]{0,1:T(8,128)} %bitcast.44) | data formatting | bytes 2097152 | tf_op jit(solution)/shard_map/reshape | solution.py:73
  20.6 1.4 %fusion.11 = bf16[512,512]{1,0:T(8,128)(2,1)S(1)} fusion(bf16[512,512]{1,0:T(8,128)(2,1)} %param.11, f32[512,512]{1,0:T(8,128)S(1)} %copy.28), kind=kLoop, calls=%fused_computation.16 | loop fusion | flops 2621440 | bytes 2097152 | tf_op jit(solution)/shard_map/convert_element_type | solution.py:76
  22.1 1.3 %collective-permute-start.1 = (bf16[3,512]{1,0:T(4,128)(2,1)S(1)}, bf16[3,512]{1,0:T(4,128)(2,1)S(1)}, u32[]{:S(2)}, u32[]{:S(2)}) collective-permute-start(bf16[3,512]{1,0:T(4,128)(2,1)S(1)} %slice.50), channel_id=1, source_target_pairs={{16,0},{17,1},{18,2},{19,3},{20,4},{21,5},{22,6},{23,7},{24,8},{25... | collective-permute-start | bytes 9224 | tf_op jit(solution)/shard_map/ppermute | solution.py:14
  23.4 2.1 %collective-permute-done.1 = bf16[3,512]{1,0:T(4,128)(2,1)S(1)} collective-permute-done((bf16[3,512]{1,0:T(4,128)(2,1)S(1)}, bf16[3,512]{1,0:T(4,128)(2,1)S(1)}, u32[]{:S(2)}, u32[]{:S(2)}) %collective-permute-start.1) | collective-permute-done | bytes 3104 | tf_op jit(solution)/shard_map/ppermute | solution.py:14
  25.5 0.1 maximum_convert_fusion
  25.7 1.3 %fusion.13 = bf16[512,512]{1,0:T(8,128)(2,1)} fusion(f32[515,512]{1,0:T(8,128)S(1)} %maximum_convert_fusion, f32[512]{0:T(512)S(1)} %bitcast.50, f32[512]{0:T(512)S(1)} %bitcast.51, f32[512]{0:T(512)S(1)} %bitcast.49, f32[512]{0:T(512)S(1)} %bitcast.48), kind=kLoop, calls=%fused_computation.19 | loop fusion | flops 2097152 | bytes 4726784 | tf_op jit(solution)/shard_map/convert_element_type | solution.py:82
  27.0 48.4 %all-gather.2.cloned.1.call-done = bf16[512,2048]{1,0:T(8,128)(2,1)} async-done(((bf16[512,512]{1,0:T(8,128)(2,1)}), bf16[512,2048]{1,0:T(8,128)(2,1)}) %all-gather.2.cloned.1.call-update) | async-done | bytes 2097168 | tf_op jit(solution)/shard_map/all_gather | solution.py:84
  75.4 9.9 %convolution_convert_fusion = bf16[512,2048]{1,0:T(8,128)(2,1)} fusion(bf16[512,2048]{1,0:T(8,128)(2,1)} %all-gather.2.cloned.1.call-done, bf16[2048,2048]{1,0:T(8,128)(2,1)} %param.19), kind=kOutput, calls=%fused_computation.3 | convolution fusion | flops 4296015872 | bytes 12582912 | tf_op jit(solution)/shard_map/dot_general | solution.py:83
  85.3 0.9 add_bitcast_fusion
  86.2 33.2 %reduce-scatter.2.cloned.1.call-done = bf16[512,512]{1,0:T(8,128)(2,1)} async-done(((bf16[512,2048]{1,0:T(8,128)(2,1)}), bf16[512,512]{1,0:T(8,128)(2,1)}) %reduce-scatter.2.cloned.1.call-update) | async-done | bytes 524304 | tf_op jit(solution)/shard_map/reduce_scatter | solution.py:89
  (23 shorter events, 0.3 us)
Async XLA Ops:
  7.2 4.2 %copy-start = (bf16[512,4,256]{2,1,0:T(4,128)(2,1)S(1)}, bf16[512,4,256]{2,1,0:T(4,128)(2,1)}, u32[]{:S(2)}) copy-start(bf16[512,4,256]{2,1,0:T(4,128)(2,1)} %param.13) | copy-start | bytes 3145732
  7.2 68.2 %all-gather.2.cloned.1.call-start = ((), (), s32[]{:S(2)}) async-start(), calls=%async_computation.1 | async-start | bytes 2621440 | tf_op jit(solution)/shard_map/all_gather | solution.py:84
  11.3 2.4 %copy-start.2 = (bf16[512,4,256]{2,1,0:T(4,128)(2,1)S(1)}, bf16[512,4,256]{2,1,0:T(4,128)(2,1)}, u32[]{:S(2)}) copy-start(bf16[512,4,256]{2,1,0:T(4,128)(2,1)} %param.12) | copy-start | bytes 3145732
  12.3 5.0 %collective-permute-start = (bf16[8,64,256]{2,1,0:T(8,128)(2,1)S(1)}, bf16[8,64,256]{2,1,0:T(8,128)(2,1)S(1)}, u32[]{:S(2)}, u32[]{:S(2)}) collective-permute-start(bf16[8,64,256]{2,1,0:T(8,128)(2,1)S(1)} %get-tuple-element.27), channel_id=1, source_target_pairs={{16,0},{17,1},{18,2},{19,3},{20,4},{21,5},{22,6},{23,7},{24,8},{25... | collective-permute-start | bytes 786440 | tf_op jit(solution)/shard_map/while/body/eval_jaxpr/ppermute | solution.py:14
  14.6 2.7 %copy-start.1 = (f32[8,64,256]{2,1,0:T(8,128)S(1)}, f32[8,64,256]{2,1,0:T(8,128)}, u32[]{:S(2)}) copy-start(f32[8,64,256]{2,1,0:T(8,128)} %param.18) | copy-start | bytes 1572868
  14.6 2.7 %copy-start.3 = (f32[8,512]{1,0:T(8,128)S(1)}, f32[8,512]{1,0:T(8,128)}, u32[]{:S(2)}) copy-start(f32[8,512]{1,0:T(8,128)} %param.14) | copy-start | bytes 49156
  14.6 2.7 %copy-start.5 = (f32[8]{0:T(128)S(1)}, f32[8]{0:T(128)}, u32[]{:S(2)}) copy-start(f32[8]{0:T(128)} %param.16) | copy-start | bytes 100
  17.2 6.2 %copy-start.4 = (f32[4,512]{1,0:T(4,128)S(1)}, f32[4,512]{1,0:T(4,128)}, u32[]{:S(2)}) copy-start(f32[4,512]{1,0:T(4,128)} %param.17) | copy-start | bytes 24580
  22.1 3.4 %collective-permute-start.1 = (bf16[3,512]{1,0:T(4,128)(2,1)S(1)}, bf16[3,512]{1,0:T(4,128)(2,1)S(1)}, u32[]{:S(2)}, u32[]{:S(2)}) collective-permute-start(bf16[3,512]{1,0:T(4,128)(2,1)S(1)} %slice.50), channel_id=1, source_target_pairs={{16,0},{17,1},{18,2},{19,3},{20,4},{21,5},{22,6},{23,7},{24,8},{25... | collective-permute-start | bytes 9224 | tf_op jit(solution)/shard_map/ppermute | solution.py:14
  27.0 92.4 %reduce-scatter.2.cloned.1.call-start = ((), (), s32[]{:S(2)}) async-start(), calls=%async_computation.2 | async-start | bytes 2621440 | tf_op jit(solution)/shard_map/reduce_scatter | solution.py:89
Sparse Core Ops, SparseCore 0:
  27.1 48.2 all-gather.1
  85.4 33.9 reduce-scatter.1
where the time goes:
time: 127 us; the launch traced here: 126 us
  waiting for transfers between devices  83.7 us (66%)
  matrix products  14.8 us (12%)
  between operations  14.3 us (11%)
  other arithmetic  6.41 us (5%)
  local copies, waits for them, and re-layouts  4.32 us (3%)
  starting transfers between devices  2.66 us (2%)
    all_gather x1, waiting for transfers between devices, on_device(): lax.all_gather(x_grad, 'col', axis=1, tiled=True)  48.4 us
    reduce_scatter x1, waiting for transfers between devices, on_device(): lax.psum_scatter(partial_grad.astype(jnp.bfloat16), 'row', scatter_dimens...  33.2 us
    dot_general x1, matrix products, on_device(): lax.dot_general(lax.all_gather(x_grad, 'col', axis=1, tiled=True), proj_w...  9.86 us
    ppermute x2, starting transfers between devices, from_behind(): lax.ppermute(value, axis, [(source, source + steps) for source in range(f...  2.58 us
    dot_general x1, matrix products, on_device(): jnp.einsum('hts,shd->thd', mixing, per_head, preferred_element_type=jnp.f...  2.56 us
  transfers between devices with their start and end apart: 4, of which 3 were waited for; matrix products, arithmetic and copies ran while one was open for 4% of the time, Pallas kernels for 0%

commit v1 on v0

--- a/solution.py
+++ b/solution.py
@@ -1,17 +1,217 @@
+import functools
+
 import jax
 import jax.numpy as jnp
 from jax import lax
+from jax.experimental import pallas as pl
+from jax.experimental.pallas import tpu as pltpu
 from jax.sharding import PartitionSpec as P
 
 HD = 64
 HPG = 32
 KW = 4
+CHUNKS = 4
+REACH = 2
 
 
 def from_behind(value, axis, steps):
     count = lax.axis_size(axis)
     first, last = (max(0, -steps), min(count, count - steps))
     return lax.ppermute(value, axis, [(source, source + steps) for source in range(first, last)])
+
+
+def project_kernel(
+    n_row,
+    n_col,
+    x_ref,
+    w_hbm,
+    out_ref,
+    w_ref,
+    gathered,
+    staged,
+    landed,
+    own,
+    w_sem,
+    col_send,
+    col_recv,
+    fwd_send,
+    row_send,
+    row_recv,
+):
+    row = lax.axis_index("row")
+    col = lax.axis_index("col")
+    step = gathered.shape[2]
+    width = gathered.shape[3]
+    d_out = out_ref.shape[1]
+    mesh_id = pl.DeviceIdType.MESH
+
+    load_w = pltpu.make_async_copy(w_hbm, w_ref, w_sem)
+    load_w.start()
+
+    barrier = pltpu.get_barrier_semaphore()
+    for j in range(1, n_row):
+        pl.semaphore_signal(
+            barrier, inc=1, device_id={"row": lax.rem(row + j, n_row)}, device_id_type=mesh_id
+        )
+    for j in range(1, n_col):
+        pl.semaphore_signal(
+            barrier, inc=1, device_id={"col": lax.rem(col + j, n_col)}, device_id_type=mesh_id
+        )
+    pl.semaphore_wait(barrier, n_row + n_col - 2)
+
+    deltas = [d for d in range(-REACH, REACH + 1) if d != 0]
+
+    def col_copy(chunk, owner, target, sem):
+        return pltpu.make_async_remote_copy(
+            src_ref=gathered.at[chunk, owner],
+            dst_ref=gathered.at[chunk, owner],
+            send_sem=sem,
+            recv_sem=col_recv.at[chunk, owner],
+            device_id={"col": target},
+            device_id_type=mesh_id,
+        )
+
+    def each_send(chunk, act):
+        for at, delta in enumerate(deltas):
+            target = col + delta
+
+            @pl.when((target >= 0) & (target < n_col))
+            def _():
+                act(col_copy(chunk, col, target, col_send.at[chunk, at]))
+
+    def send_chunk(chunk):
+        gathered[chunk, col] = x_ref[pl.ds(pl.multiple_of(chunk * step, step), step), :]
+        each_send(chunk, lambda copy: copy.start())
+
+    def each_arrival(chunk, receive, forward):
+        for side, sign in enumerate((-1, 1)):
+            for dist in list(range(REACH, n_col)) + list(range(1, REACH)):
+                owner = col + sign * dist
+
+                @pl.when((owner >= 0) & (owner < n_col))
+                def _():
+                    if receive:
+                        col_copy(chunk, owner, col, fwd_send.at[chunk, side, dist]).wait_recv()
+                    if dist >= REACH:
+                        target = col - sign
+
+                        @pl.when((target >= 0) & (target < n_col))
+                        def _():
+                            forward(
+                                col_copy(chunk, owner, target, fwd_send.at[chunk, side, dist])
+                            )
+
+    def row_copy(chunk, target):
+        return pltpu.make_async_remote_copy(
+            src_ref=staged.at[chunk, target],
+            dst_ref=landed.at[chunk, row],
+            send_sem=row_send.at[chunk, target],
+            recv_sem=row_recv.at[chunk, row],
+            device_id={"row": target},
+            device_id_type=mesh_id,
+        )
+
+    def finish(chunk):
+        total = own[chunk]
+        for j in range(1, n_row):
+            source = lax.rem(row + j, n_row)
+            pltpu.make_async_remote_copy(
+                src_ref=staged.at[chunk, source],
+                dst_ref=landed.at[chunk, source],
+                send_sem=row_send.at[chunk, source],
+                recv_sem=row_recv.at[chunk, source],
+                device_id={"row": source},
+                device_id_type=mesh_id,
+            ).wait_recv()
+            total = total + landed[chunk, source].astype(jnp.float32)
+        out_ref[pl.ds(pl.multiple_of(chunk * step, step), step), :] = total.astype(out_ref.dtype)
+
+    def product(chunk, target):
+        rows = pl.ds(pl.multiple_of(target * d_out, d_out), d_out)
+        total = None
+        for owner in range(n_col):
+            part = lax.dot_general(
+                gathered[chunk, owner],
+                w_ref[rows, owner * width : (owner + 1) * width],
+                (((1,), (1,)), ((), ())),
+                preferred_element_type=jnp.float32,
+            )
+            total = part if total is None else total + part
+        return total
+
+    send_chunk(0)
+    send_chunk(1)
+    load_w.wait()
+
+    def turn(chunk, carry):
+        each_arrival(chunk, True, lambda copy: copy.start())
+        each_send(chunk, lambda copy: copy.wait_send())
+
+        @pl.when(chunk + 2 < CHUNKS)
+        def _():
+            send_chunk(chunk + 2)
+
+        @pl.loop(1, n_row)
+        def _(j):
+            target = lax.rem(row + j, n_row)
+            staged[chunk, target] = product(chunk, target).astype(jnp.bfloat16)
+            row_copy(chunk, target).start()
+
+        own[chunk] = product(chunk, row)
+
+        @pl.when(chunk > 0)
+        def _():
+            finish(chunk - 1)
+
+        return carry
+
+    lax.fori_loop(0, CHUNKS, turn, 0)
+    finish(CHUNKS - 1)
+
+    def drain(chunk, carry):
+        each_arrival(chunk, False, lambda copy: copy.wait_send())
+        for j in range(1, n_row):
+            row_copy(chunk, lax.rem(row + j, n_row)).wait_send()
+        return carry
+
+    lax.fori_loop(0, CHUNKS, drain, 0)
+
+
+def project(x_grad, proj_weight):
+    n_row, n_col = lax.axis_size("row"), lax.axis_size("col")
+    tokens, width = x_grad.shape
+    step = tokens // CHUNKS
+    d_out = proj_weight.shape[0] // n_row
+    return pl.pallas_call(
+        functools.partial(project_kernel, n_row, n_col),
+        out_shape=jax.ShapeDtypeStruct((tokens, d_out), jnp.bfloat16),
+        in_specs=[
+            pl.BlockSpec(memory_space=pltpu.VMEM),
+            pl.BlockSpec(memory_space=pl.ANY),
+        ],
+        out_specs=pl.BlockSpec(memory_space=pltpu.VMEM),
+        scratch_shapes=[
+            pltpu.VMEM(proj_weight.shape, jnp.bfloat16),
+            pltpu.VMEM((CHUNKS, n_col, step, width), jnp.bfloat16),
+            pltpu.VMEM((CHUNKS, n_row, step, d_out), jnp.bfloat16),
+            pltpu.VMEM((CHUNKS, n_row, step, d_out), jnp.bfloat16),
+            pltpu.VMEM((CHUNKS, step, d_out), jnp.float32),
+            pltpu.SemaphoreType.DMA,
+            pltpu.SemaphoreType.DMA((CHUNKS, 2 * REACH)),
+            pltpu.SemaphoreType.DMA((CHUNKS, n_col)),
+            pltpu.SemaphoreType.DMA((CHUNKS, 2, n_col)),
+            pltpu.SemaphoreType.DMA((CHUNKS, n_row)),
+            pltpu.SemaphoreType.DMA((CHUNKS, n_row)),
+        ],
+        compiler_params=pltpu.CompilerParams(
+            collective_id=0, has_side_effects=True, vmem_limit_bytes=48 << 20
+        ),
+        cost_estimate=pl.CostEstimate(
+            flops=2 * tokens * proj_weight.shape[0] * proj_weight.shape[1],
+            bytes_accessed=2 * proj_weight.shape[0] * proj_weight.shape[1],
+            transcendentals=0,
+        ),
+    )(x_grad, proj_weight)
 
 
 def on_device(
@@ -80,15 +280,7 @@
     for tap in range(KW):
         accum = accum + conv_weight[tap][None, :] * extended[tap : tap + tokens_dev]
     x_grad = accum.astype(jnp.bfloat16)
-    partial_grad = lax.dot_general(
-        lax.all_gather(x_grad, "col", axis=1, tiled=True),
-        proj_weight,
-        (((1,), (1,)), ((), ())),
-        preferred_element_type=jnp.float32,
-    )
-    hidden_grad = lax.psum_scatter(
-        partial_grad.astype(jnp.bfloat16), "row", scatter_dimension=1, tiled=True
-    )
+    hidden_grad = project(x_grad, proj_weight)
     return (hidden_grad, x_grad, state_start[None])
 
 

time: 127 us -> 76.2 us (0.60)
  waiting for transfers between devices: 83.7 us -> 0.19 us
  Pallas kernels: 0 us -> 53.2 us
  between operations: 14.3 us -> 0.83 us
  matrix products: 14.8 us -> 5.8 us
  local copies, waits for them, and re-layouts: 4.32 us -> 6.33 us
    pallas_call x0 -> x1, Pallas kernels: none -> 53.2 us  [project(): pl.pallas_call(functools.partial(project_kernel, n_row, n_col), out_shape...]
    all_gather x1 -> x0, waiting for transfers between devices: 48.4 us -> none  [on_device(): lax.all_gather(x_grad, 'col', axis=1, tiled=True)]
    reduce_scatter x1 -> x0, waiting for transfers between devices: 33.2 us -> none  [on_device(): lax.psum_scatter(partial_grad.astype(jnp.bfloat16), 'row', scatter_dimens...]
    dot_general x1 -> x0, matrix products: 9.86 us -> none  [on_device(): lax.dot_general(lax.all_gather(x_grad, 'col', axis=1, tiled=True), proj_w...]
    ppermute x2, waiting for transfers between devices: 2.12 us -> 0.19 us  [from_behind(): lax.ppermute(value, axis, [(source, source + steps) for source in range(f...]
  transfers between devices with their start and end apart: 4 -> 2, of which waited for: 3 -> 1; matrix products, arithmetic and copies ran while one was open for 4% -> 9% of each run, Pallas kernels for 0% -> 0%
where the time goes in v1:
time: 76.2 us; the launch traced here: 75.7 us
  Pallas kernels  53.2 us (70%)
  other arithmetic  6.66 us (9%)
  local copies, waits for them, and re-layouts  6.33 us (8%)
  matrix products  5.8 us (8%)
  starting transfers between devices  2.72 us (4%)
  between operations  0.83 us (1%)
    pallas_call x1, Pallas kernels, project(): pl.pallas_call(functools.partial(project_kernel, n_row, n_col), out_shape...  53.2 us
    ppermute x2, starting transfers between devices, from_behind(): lax.ppermute(value, axis, [(source, source + steps) for source in range(f...  2.72 us
    dot_general x1, matrix products, on_device(): jnp.einsum('hts,shd->thd', mixing, per_head, preferred_element_type=jnp.f...  2.56 us
    another operation x2, other arithmetic  2.33 us
    unnamed x14, local copies, waits for them, and re-layouts  2.09 us
    broadcast_in_dim x1, other arithmetic, on_device(): return (hidden_grad, x_grad, state_start[None])  1.96 us
    dot_general x1, matrix products, on_device(): jnp.einsum('hdn,tn->thd', carried, write_rows.astype(jnp.float32), precis...  1.79 us
    dynamic_slice x1, local copies, waits for them, and re-layouts, on_device(): write_rows = lax.dynamic_index_in_dim(input_mix, group, 1, keepdims=False)  1.77 us
  transfers between devices with their start and end apart: 2, of which 1 were waited for; matrix products, arithmetic and copies ran while one was open for 9% of the time, Pallas kernels for 0%

profile of v1, /device:TPU:0, one launch (start us, length us, event | category | flops | bytes accessed | tf_op | source)
XLA Modules:
  0.0 75.7 jit_solution(14119055139914963810)
XLA Ops:
  0.7 2.3 %reduce-window.6 = f32[8,4,128]{2,0,1:T(8,128)S(1)} reduce-window(f32[8,4,128]{2,0,1:T(8,128)} %bitcast.45, f32[]{:T(128)} %constant.39.clone.1), window={size=1x1x128 pad=0_0x0_0x127_0}, to_apply=%region_0.1 | reduce-window | flops 520192 | bytes 32772 | tf_op jit(solution)/shard_map/reduce-window
  3.0 0.2 slice_reduce_fusion
  3.2 0.1 exponential_bitcast_fusion.1
  3.2 1.3 %copy.26 = bf16[512,512]{0,1:T(8,128)(2,1)S(1)} copy(bf16[512,512]{1,0:T(8,128)(2,1)} %param.10) | data formatting | bytes 1048576 | tf_op args[0]
  4.5 0.2 slice_reduce_fusion.1
  4.7 0.5 constant_dynamic-slice_fusion
  5.3 0.1 fusion.16
  5.4 1.1 %add_convert_fusion = (bf16[8,64,256]{2,1,0:T(8,128)(2,1)S(1)}, f32[8,64,256]{2,1,0:T(8,128)}) fusion(f32[8,64,256]{2,1,0:T(8,128)} %param.18, f32[8]{0:T(128)S(1)} %exp.21, pred[]{:T(512)S(6)} %eq.3, bf16[512,8,64]{0,2,1:T(8,128)(2,1)S(1)} %bitcast.43, bf16[512,1,256]{2,1,0:T(2,128)(2,1)S(1)} %constant_dynamic-slice_fusion), kind=kOutput, calls=%fused_computation.30 | convolution fusion | flops 134742016 | bytes 2097185 | tf_op jit(solution)/shard_map/shd,sn->hdn/dot_general | solution.py:242
  6.5 1.4 %collective-permute-start = (bf16[8,64,256]{2,1,0:T(8,128)(2,1)S(1)}, bf16[8,64,256]{2,1,0:T(8,128)(2,1)S(1)}, u32[]{:S(2)}, u32[]{:S(2)}) collective-permute-start(bf16[8,64,256]{2,1,0:T(8,128)(2,1)S(1)} %get-tuple-element.27), channel_id=1, source_target_pairs={{16,0},{17,1},{18,2},{19,3},{20,4},{21,5},{22,6},{23,7},{24,8},{25... | collective-permute-start | bytes 786440 | tf_op jit(solution)/shard_map/while/body/eval_jaxpr/ppermute | solution.py:20
  7.9 0.1 iota_compare_fusion
  8.0 1.8 %constant_dynamic-slice_fusion.1 = bf16[512,1,256]{2,1,0:T(2,128)(2,1)S(1)} fusion(bf16[512,4,256]{2,1,0:T(4,128)(2,1)} %param.12, s32[]{:T(128)S(6)} %select_n.30), kind=kLoop, calls=%fused_computation.48 | loop fusion | bytes 524292 | tf_op jit(solution)/shard_map/jit(dynamic_index_in_dim)/dynamic_slice | solution.py:233
  9.8 0.3 fusion.20
  10.1 2.6 %fusion.2 = f32[512,8,64]{0,2,1:T(8,128)S(1)} fusion(bf16[512,8,64]{0,2,1:T(8,128)(2,1)S(1)} %bitcast.40, f32[512,512]{1,0:T(8,128)S(1)} %fusion.20, f32[8,512]{1,0:T(8,128)S(1)} %get-tuple-element.16, pred[512,512]{1,0:T(8,128)(4,1)S(1)} %iota_compare_fusion), kind=kOutput, calls=%fused_computation.3 | convolution fusion | flops 276824064 | bytes 2899968 | tf_op jit(solution)/shard_map/hts,shd->thd/dot_general | solution.py:265
  12.7 0.1 exponential_bitcast_fusion
  12.8 1.8 %fusion.5 = f32[512,8,64]{0,2,1:T(8,128)} fusion(f32[512,8,64]{0,2,1:T(8,128)S(1)} %fusion.2, bf16[512,8,64]{0,2,1:T(8,128)(2,1)S(1)} %bitcast.41, f32[8]{0:T(128)S(1)} %copy-done.5, f32[512,8]{0,1:T(8,128)S(1)} %exponential_bitcast_fusion, f32[512,8]{0,1:T(8,128)S(1)} %bitcast.44, f32[8,64,256]{2,1,0:T(8,128)S(1)} %copy-done.2, ...), kind=kOutput, calls=%fused_computation.7 | convolution fusion | flops 807141376 | bytes 3702817 | tf_op jit(solution)/shard_map/hdn,tn->thd/dot_general | solution.py:266
  14.6 1.6 %copy.28 = f32[512,512]{1,0:T(8,128)S(1)} copy(f32[512,512]{0,1:T(8,128)} %bitcast.42) | data formatting | bytes 2097152 | tf_op jit(solution)/shard_map/reshape | solution.py:273
  16.2 1.4 %fusion.11 = bf16[512,512]{1,0:T(8,128)(2,1)S(1)} fusion(bf16[512,512]{1,0:T(8,128)(2,1)} %param.11, f32[512,512]{1,0:T(8,128)S(1)} %copy.28), kind=kLoop, calls=%fused_computation.15 | loop fusion | flops 2621440 | bytes 2097152 | tf_op jit(solution)/shard_map/convert_element_type | solution.py:276
  17.7 1.3 %collective-permute-start.1 = (bf16[3,512]{1,0:T(4,128)(2,1)S(1)}, bf16[3,512]{1,0:T(4,128)(2,1)S(1)}, u32[]{:S(2)}, u32[]{:S(2)}) collective-permute-start(bf16[3,512]{1,0:T(4,128)(2,1)S(1)} %slice.50), channel_id=1, source_target_pairs={{16,0},{17,1},{18,2},{19,3},{20,4},{21,5},{22,6},{23,7},{24,8},{25... | collective-permute-start | bytes 9224 | tf_op jit(solution)/shard_map/ppermute | solution.py:20
  19.0 2.0 %add_bitcast_fusion = f32[1,8,64,256]{3,2,1,0:T(8,128)} fusion(f32[8,64,256]{2,1,0:T(8,128)} %get-tuple-element.28, f32[8,64,256]{2,1,0:T(8,128)S(1)} %copy-done.2, bf16[8,64,256]{2,1,0:T(8,128)(2,1)S(1)} %collective-permute-done, f32[8]{0:T(128)S(1)} %exp.21, pred[]{:T(512)S(6)} %eq.3), kind=kLoop, calls=%fused_computation.28 | loop fusion | flops 524288 | bytes 1835041 | tf_op jit(solution)/shard_map/broadcast_in_dim | solution.py:284
  20.9 0.2 collective-permute-done.1
  21.1 0.1 maximum_convert_fusion
  21.2 0.5 fusion.13.x_ref
  21.7 53.2 %shard_map.121 = bf16[512,512]{1,0:T(8,128)(2,1)S(1)} custom-call(bf16[512,512]{1,0:T(8,128)(2,1)S(1)} %fusion.13.x_ref, bf16[2048,2048]{1,0:T(8,128)(2,1)} %w_hbm.1), custom_call_target="tpu_custom_call" | custom-call | flops 4294967296 | bytes 8388608 | tf_op jit(solution)/shard_map/pallas_call | solution.py:185
  75.0 0.8 %copy.50 = bf16[512,512]{1,0:T(8,128)(2,1)} copy(bf16[512,512]{1,0:T(8,128)(2,1)S(1)} %shard_map.121) | data formatting | bytes 1048576
  (18 shorter events, 0.1 us)
Async XLA Ops:
  0.6 4.1 %copy-start = (bf16[512,4,256]{2,1,0:T(4,128)(2,1)S(1)}, bf16[512,4,256]{2,1,0:T(4,128)(2,1)}, u32[]{:S(2)}) copy-start(bf16[512,4,256]{2,1,0:T(4,128)(2,1)} %param.13) | copy-start | bytes 3145732
  6.5 6.2 %copy-start.4 = (f32[4,512]{1,0:T(4,128)S(1)}, f32[4,512]{1,0:T(4,128)}, u32[]{:S(2)}) copy-start(f32[4,512]{1,0:T(4,128)} %param.17) | copy-start | bytes 24580
  6.5 6.3 %copy-start.2 = (f32[8,64,256]{2,1,0:T(8,128)S(1)}, f32[8,64,256]{2,1,0:T(8,128)}, u32[]{:S(2)}) copy-start(f32[8,64,256]{2,1,0:T(8,128)} %param.18) | copy-start | bytes 1572868
  6.5 6.3 %copy-start.3 = (f32[8,512]{1,0:T(8,128)S(1)}, f32[8,512]{1,0:T(8,128)}, u32[]{:S(2)}) copy-start(f32[8,512]{1,0:T(8,128)} %param.14) | copy-start | bytes 49156
  6.5 6.3 %copy-start.5 = (f32[8]{0:T(128)S(1)}, f32[8]{0:T(128)}, u32[]{:S(2)}) copy-start(f32[8]{0:T(128)} %param.16) | copy-start | bytes 100
  6.5 6.3 %collective-permute-start = (bf16[8,64,256]{2,1,0:T(8,128)(2,1)S(1)}, bf16[8,64,256]{2,1,0:T(8,128)(2,1)S(1)}, u32[]{:S(2)}, u32[]{:S(2)}) collective-permute-start(bf16[8,64,256]{2,1,0:T(8,128)(2,1)S(1)} %get-tuple-element.27), channel_id=1, source_target_pairs={{16,0},{17,1},{18,2},{19,3},{20,4},{21,5},{22,6},{23,7},{24,8},{25... | collective-permute-start | bytes 786440 | tf_op jit(solution)/shard_map/while/body/eval_jaxpr/ppermute | solution.py:20
  17.7 3.4 %collective-permute-start.1 = (bf16[3,512]{1,0:T(4,128)(2,1)S(1)}, bf16[3,512]{1,0:T(4,128)(2,1)S(1)}, u32[]{:S(2)}, u32[]{:S(2)}) collective-permute-start(bf16[3,512]{1,0:T(4,128)(2,1)S(1)} %slice.50), channel_id=1, source_target_pairs={{16,0},{17,1},{18,2},{19,3},{20,4},{21,5},{22,6},{23,7},{24,8},{25... | collective-permute-start | bytes 9224 | tf_op jit(solution)/shard_map/ppermute | solution.py:20
  21.7 54.0 %copy-start.1 = (bf16[512,512]{1,0:T(8,128)(2,1)}, bf16[512,512]{1,0:T(8,128)(2,1)S(1)}, u32[]{:S(2)}) copy-start(bf16[512,512]{1,0:T(8,128)(2,1)S(1)} %fusion.13.x_ref) | copy-start | bytes 1572868

commit v2 on v1

v2 whole, which is shorter than its diff:
```python
import functools

import jax
import jax.numpy as jnp
from jax import lax
from jax.experimental import pallas as pl
from jax.experimental.pallas import tpu as pltpu
from jax.sharding import PartitionSpec as P

HD = 64
HPG = 32
KW = 4
CHUNKS = 4
REACH = 2
FLYING = 2
RIM = 16


def layer_kernel(
    n_ctx,
    n_row,
    n_col,
    grad_ref,
    conv_ref,
    write_ref,
    read_ref,
    step_ref,
    decay_ref,
    skip_ref,
    tap_ref,
    later_ref,
    w_hbm,
    out_ref,
    x_ref,
    state_ref,
    w_ref,
    pre_ref,
    carried_ref,
    state_out,
    state_in,
    rim_out,
    rim_in,
    gathered,
    staged,
    landed,
    own,
    w_sem,
    col_send,
    col_recv,
    fwd_send,
    row_send,
    row_recv,
    ctx_send,
    ctx_recv,
):
    ctx = lax.axis_index("ctx")
    row = lax.axis_index("row")
    col = lax.axis_index("col")
    step = gathered.shape[2]
    width = gathered.shape[3]
    d_out = out_ref.shape[1]
    mesh_id = pl.DeviceIdType.MESH

    load_w = pltpu.make_async_copy(w_hbm, w_ref, w_sem)
    load_w.start()

    barrier = pltpu.get_barrier_semaphore()
    for j in range(1, n_row):
        pl.semaphore_signal(
            barrier, inc=1, device_id={"row": lax.rem(row + j, n_row)}, device_id_type=mesh_id
        )
    for j in range(1, n_col):
        pl.semaphore_signal(
            barrier, inc=1, device_id={"col": lax.rem(col + j, n_col)}, device_id_type=mesh_id
        )
    has_next, has_previous = ctx < n_ctx - 1, ctx > 0
    for there, delta in ((has_next, 1), (has_previous, -1)):

        @pl.when(there)
        def _():
            pl.semaphore_signal(
                barrier, inc=1, device_id={"ctx": ctx + delta}, device_id_type=mesh_id
            )

    deltas = [d for d in range(-REACH, REACH + 1) if d != 0]

    def col_copy(chunk, owner, target, sem):
        return pltpu.make_async_remote_copy(
            src_ref=gathered.at[chunk, owner],
            dst_ref=gathered.at[chunk, owner],
            send_sem=sem,
            recv_sem=col_recv.at[chunk, owner],
            device_id={"col": target},
            device_id_type=mesh_id,
        )

    def each_send(chunk, act):
        for at, delta in enumerate(deltas):
            target = col + delta

            @pl.when((target >= 0) & (target < n_col))
            def _():
                act(col_copy(chunk, col, target, col_send.at[chunk, at]))

    def send_chunk(chunk):
        each_send(chunk, lambda copy: copy.start())

    def each_arrival(chunk, receive, forward):
        for side, sign in enumerate((-1, 1)):
            for dist in list(range(REACH, n_col)) + list(range(1, REACH)):
                owner = col + sign * dist

                @pl.when((owner >= 0) & (owner < n_col))
                def _():
                    if receive:
                        col_copy(chunk, owner, col, fwd_send.at[chunk, side, dist]).wait_recv()
                    if dist >= REACH:
                        target = col - sign

                        @pl.when((target >= 0) & (target < n_col))
                        def _():
                            forward(
                                col_copy(chunk, owner, target, fwd_send.at[chunk, side, dist])
                            )

    def row_copy(chunk, target):
        return pltpu.make_async_remote_copy(
            src_ref=staged.at[chunk, target],
            dst_ref=landed.at[chunk, row],
            send_sem=row_send.at[chunk, target],
            recv_sem=row_recv.at[chunk, row],
            device_id={"row": target},
            device_id_type=mesh_id,
        )

    def finish(chunk):
        total = own[chunk]
        for j in range(1, n_row):
            source = lax.rem(row + j, n_row)
            pltpu.make_async_remote_copy(
                src_ref=staged.at[chunk, source],
                dst_ref=landed.at[chunk, source],
                send_sem=row_send.at[chunk, source],
                recv_sem=row_recv.at[chunk, source],
                device_id={"row": source},
                device_id_type=mesh_id,
            ).wait_recv()
            total = total + landed[chunk, source].astype(jnp.float32)
        first = pl.multiple_of((CHUNKS - 1 - chunk) * step, step)
        out_ref[pl.ds(first, step), :] = total.astype(out_ref.dtype)

    def product(chunk, target):
        rows = pl.ds(pl.multiple_of(target * d_out, d_out), d_out)
        total = None
        for owner in range(n_col):
            part = lax.dot_general(
                gathered[chunk, owner],
                w_ref[rows, owner * width : (owner + 1) * width],
                (((1,), (1,)), ((), ())),
                preferred_element_type=jnp.float32,
            )
            total = part if total is None else total + part
        return total

    def ctx_copy(at, source, target):
        return pltpu.make_async_remote_copy(
            src_ref=source,
            dst_ref=target,
            send_sem=ctx_send.at[at],
            recv_sem=ctx_recv.at[at],
            device_id={"ctx": lax.rem(ctx + n_ctx - 1, n_ctx)},
            device_id_type=mesh_id,
        )

    pass_state = ctx_copy(0, state_out, state_in)
    pass_rim = ctx_copy(1, rim_out, rim_in)

    tokens = grad_ref.shape[0]
    heads = decay_ref.shape[0]
    pairs = heads // 2
    lanes = 2 * HD
    f32, bf16 = jnp.float32, jnp.bfloat16

    def dot(a, b, a_dim, b_dim):
        return lax.dot_general(
            a, b, (((a_dim,), (b_dim,)), ((), ())), preferred_element_type=f32
        )

    decay = decay_ref[...]
    high = decay.astype(bf16)
    rest = decay - high.astype(f32)
    middle = rest.astype(bf16)
    low = (rest - middle.astype(f32)).astype(bf16)
    upto = lax.broadcasted_iota(jnp.int32, (tokens, tokens), 0) <= lax.broadcasted_iota(
        jnp.int32, (tokens, tokens), 1
    )
    triangle = upto.astype(f32).astype(bf16)
    cumulative = (
        dot(high, triangle, 1, 0) + dot(middle, triangle, 1, 0) + dot(low, triangle, 1, 0)
    )
    by_token = cumulative.T
    steps = step_ref[...].T
    grown = jnp.exp(by_token)
    left = jnp.exp(by_token[tokens - 1 : tokens, :] - by_token)

    def spread(columns, pair, count):
        lane = lax.broadcasted_iota(jnp.int32, (count, lanes), 1)
        return jnp.where(
            lane < HD, columns[:, 2 * pair : 2 * pair + 1], columns[:, 2 * pair + 1 : 2 * pair + 2]
        )

    weighted = jnp.concatenate(
        [
            (
                spread(grown, pair, tokens)
                * grad_ref[:, pair * lanes : (pair + 1) * lanes].astype(f32)
            ).astype(bf16)
            for pair in range(pairs)
        ],
        axis=1,
    )
    block_sum = dot(weighted, read_ref[...], 0, 0)

    total_signals = n_row + n_col - 2 + has_next.astype(jnp.int32) + has_previous.astype(jnp.int32)
    pl.semaphore_wait(barrier, total_signals)

    @pl.when(has_next)
    def _():
        pass_state.wait_recv()
        carried_ref[...] = state_in[...].astype(f32)

    @pl.when(jnp.logical_not(has_next))
    def _():
        carried_ref[...] = later_ref[...]

    for head in range(heads):
        rows = slice(head * HD, (head + 1) * HD)
        factor = jnp.exp(cumulative[head : head + 1, tokens - 1 : tokens])
        state = block_sum[rows] + factor * carried_ref[rows, :]
        state_ref[rows, :] = state
        state_out[rows, :] = state.astype(bf16)

    @pl.when(has_previous)
    def _():
        pass_state.start()

    carried = carried_ref[...].astype(bf16)

    def pre_rows(start, count):
        rows = slice(start, start + count)
        span = tokens - start
        write = write_ref[rows, :]
        scores = dot(write, read_ref[start:, :], 1, 1)
        later = lax.broadcasted_iota(jnp.int32, (count, span), 1) >= lax.broadcasted_iota(
            jnp.int32, (count, span), 0
        )
        scores = jnp.where(later, scores, 0.0)
        inter = dot(write, carried, 1, 1)
        lane = lax.broadcasted_iota(jnp.int32, (count, lanes), 1)
        found = []
        for pair in range(pairs):
            columns = slice(pair * lanes, (pair + 1) * lanes)
            mixing = []
            for head in (2 * pair, 2 * pair + 1):
                offset = cumulative[head : head + 1, start:] - by_token[rows, head : head + 1]
                mixing.append((jnp.exp(jnp.minimum(offset, 0.0)) * scores).astype(bf16))
            both = dot(jnp.concatenate(mixing, axis=0), grad_ref[start:, columns], 1, 0)
            intra = jnp.where(lane < HD, both[:count], both[count:])
            summed = intra + inter[:, columns] * spread(left[rows], pair, count)
            value = (
                spread(steps[rows], pair, count) * summed
                + skip_ref[:, columns] * grad_ref[rows, columns].astype(f32)
            )
            v = conv_ref[rows, columns].astype(f32)
            q = 1.0 / (1.0 + jnp.exp(-v))
            found.append((value * q * (1.0 + v * (1.0 - q))).astype(bf16))
        return jnp.concatenate(found, axis=1)

    @pl.when(has_previous)
    def _():
        rim_out[...] = pre_rows(0, RIM)
        pass_rim.start()

    for chunk in range(CHUNKS):
        start = tokens - (chunk + 1) * step
        pre_ref[start : start + step, :] = pre_rows(start, step).astype(f32)
        if chunk == 0:

            @pl.when(has_next)
            def _():
                pass_rim.wait_recv()
                pre_ref[tokens:, :] = rim_in[...].astype(f32)

            @pl.when(jnp.logical_not(has_next))
            def _():
                pre_ref[tokens:, :] = jnp.zeros((RIM, pre_ref.shape[1]), f32)

        mixed = tap_ref[0:1, :] * pre_ref[start : start + step, :]
        for tap in range(1, KW):
            mixed = mixed + tap_ref[tap : tap + 1, :] * pre_ref[start + tap : start + tap + step, :]
        mixed = mixed.astype(bf16)
        x_ref[start : start + step, :] = mixed
        gathered[chunk, col] = mixed
        if chunk < FLYING:
            send_chunk(chunk)
    load_w.wait()

    def turn(chunk, carry):
        each_arrival(chunk, True, lambda copy: copy.start())
        each_send(chunk, lambda copy: copy.wait_send())

        @pl.when(chunk + FLYING < CHUNKS)
        def _():
            send_chunk(chunk + FLYING)

        @pl.loop(1, n_row)
        def _(j):
            target = lax.rem(row + j, n_row)
            staged[chunk, target] = product(chunk, target).astype(jnp.bfloat16)
            row_copy(chunk, target).start()

        own[chunk] = product(chunk, row)

        @pl.when(chunk > 0)
        def _():
            finish(chunk - 1)

        return carry

    lax.fori_loop(0, CHUNKS, turn, 0)
    finish(CHUNKS - 1)

    def drain(chunk, carry):
        each_arrival(chunk, False, lambda copy: copy.wait_send())
        for j in range(1, n_row):
            row_copy(chunk, lax.rem(row + j, n_row)).wait_send()
        return carry

    lax.fori_loop(0, CHUNKS, drain, 0)

    @pl.when(has_previous)
    def _():
        pass_state.wait_send()
        pass_rim.wait_send()


def on_device(
    output_grad,
    conv_out,
    input_mix,
    output_mix,
    step_size,
    log_decay,
    skip_gain,
    conv_weight,
    later_grad,
    proj_weight,
):
    n_ctx, n_row, n_col = (lax.axis_size(name) for name in ("ctx", "row", "col"))
    tokens, width = output_grad.shape
    heads = step_size.shape[0]
    states = later_grad.shape[2]
    head_block = lax.axis_index("row") * n_col + lax.axis_index("col")
    group = head_block * heads // HPG
    write_rows = lax.dynamic_index_in_dim(input_mix, group, 1, keepdims=False)
    read_rows = lax.dynamic_index_in_dim(output_mix, group, 1, keepdims=False)
    step = tokens // CHUNKS
    d_out = proj_weight.shape[0] // n_row
    in_vmem = pl.BlockSpec(memory_space=pltpu.VMEM)
    bf16, f32 = jnp.bfloat16, jnp.float32
    hidden_grad, x_grad, state_grad = pl.pallas_call(
        functools.partial(layer_kernel, n_ctx, n_row, n_col),
        out_shape=(
            jax.ShapeDtypeStruct((tokens, d_out), bf16),
            jax.ShapeDtypeStruct((tokens, width), bf16),
            jax.ShapeDtypeStruct((width, states), f32),
        ),
        in_specs=[in_vmem] * 9 + [pl.BlockSpec(memory_space=pl.ANY)],
        out_specs=(in_vmem,) * 3,
        scratch_shapes=[
            pltpu.VMEM(proj_weight.shape, bf16),
            pltpu.VMEM((tokens + RIM, width), f32),
            pltpu.VMEM((width, states), f32),
            pltpu.VMEM((width, states), bf16),
            pltpu.VMEM((width, states), bf16),
            pltpu.VMEM((RIM, width), bf16),
            pltpu.VMEM((RIM, width), bf16),
            pltpu.VMEM((CHUNKS, n_col, step, width), bf16),
            pltpu.VMEM((CHUNKS, n_row, step, d_out), bf16),
            pltpu.VMEM((CHUNKS, n_row, step, d_out), bf16),
            pltpu.VMEM((CHUNKS, step, d_out), f32),
            pltpu.SemaphoreType.DMA,
            pltpu.SemaphoreType.DMA((CHUNKS, 2 * REACH)),
            pltpu.SemaphoreType.DMA((CHUNKS, n_col)),
            pltpu.SemaphoreType.DMA((CHUNKS, 2, n_col)),
            pltpu.SemaphoreType.DMA((CHUNKS, n_row)),
            pltpu.SemaphoreType.DMA((CHUNKS, n_row)),
            pltpu.SemaphoreType.DMA((2,)),
            pltpu.SemaphoreType.DMA((2,)),
        ],
        compiler_params=pltpu.CompilerParams(
            collective_id=0, has_side_effects=True, vmem_limit_bytes=48 << 20
        ),
    )(
        output_grad,
        conv_out,
        write_rows,
        read_rows,
        step_size,
        log_decay,
        jnp.repeat(skip_gain, HD)[None, :],
        conv_weight,
        later_grad.reshape(width, states),
        proj_weight,
    )
    return (hidden_grad, x_grad, state_grad.reshape(1, heads, HD, states))


def solution(mesh):
    return jax.shard_map(
        on_device,
        mesh=mesh,
        in_specs=(
            P("ctx", ("row", "col")),
            P("ctx", ("row", "col")),
            P("ctx", None, None),
            P("ctx", None, None),
            P(("row", "col"), "ctx"),
            P(("row", "col"), "ctx"),
            P(("row", "col")),
            P(None, ("row", "col")),
            P(("row", "col"), None, None),
            P("col", "row"),
        ),
        out_specs=(
            P("ctx", ("col", "row")),
            P("ctx", ("row", "col")),
            P("ctx", ("row", "col"), None, None),
        ),
        check_vma=False,
    )
```

time: 76.2 us -> 65.3 us (0.86)
  other arithmetic: 6.66 us -> 0 us
  matrix products: 5.8 us -> 0 us
  local copies, waits for them, and re-layouts: 6.33 us -> 11.1 us
  starting transfers between devices: 2.72 us -> 0 us
    dot_general x4 -> x0, matrix products: 5.8 us -> none  [the longest x1 2.56 us: on_device(): jnp.einsum('hts,shd->thd', mixing, per_head, preferred_element_type=jnp.f...]
    unnamed x14 -> x17, local copies, waits for them, and re-layouts: 2.09 us -> 7.71 us
    ppermute x2 -> x0, starting transfers between devices: 2.72 us -> none  [from_behind(): lax.ppermute(value, axis, [(source, source + steps) for source in range(f...]
    another operation x2 -> x0, other arithmetic: 2.33 us -> none
    convert_element_type x4 -> x0, other arithmetic: 2.14 us -> none  [the longest x1 1.45 us: on_device(): (flat_grad * sigma * (1.0 + activated * (1.0 - sigma))).astype(jnp.bfloat16)]
    dynamic_slice x1, local copies, waits for them, and re-layouts: 0.55 us -> 2.62 us  [on_device(): read_rows = lax.dynamic_index_in_dim(output_mix, group, 1, keepdims=False)]
    broadcast_in_dim x1 -> x0, other arithmetic: 1.96 us -> none  [on_device(): return (hidden_grad, x_grad, state_start[None])]
    dynamic_slice x1 -> x0, local copies, waits for them, and re-layouts: 1.77 us -> none  [on_device(): write_rows = lax.dynamic_index_in_dim(input_mix, group, 1, keepdims=False)]
  transfers between devices with their start and end apart: 2 -> 0, of which waited for: 1 -> 0; matrix products, arithmetic and copies ran while one was open for 9% -> 0% of each run, Pallas kernels for 0% -> 0%
where the time goes in v2:
time: 65.3 us; the launch traced here: 64.8 us
  Pallas kernels  53 us (81%)
  local copies, waits for them, and re-layouts  11.1 us (17%)
  between operations  0.69 us (1%)
    pallas_call x1, Pallas kernels, on_device(): pl.pallas_call(functools.partial(layer_kernel, n_ctx, n_row, n_col), out_...  53 us
    unnamed x17, local copies, waits for them, and re-layouts  7.71 us
    dynamic_slice x1, local copies, waits for them, and re-layouts, on_device(): read_rows = lax.dynamic_index_in_dim(output_mix, group, 1, keepdims=False)  2.62 us

profile of v2, /device:TPU:0, one launch (start us, length us, event | category | flops | bytes accessed | tf_op | source)
XLA Modules:
  0.0 64.8 jit_solution(18017544935649468210)
XLA Ops:
  0.7 0.7 %broadcast_in_dim.3 = f32[8,64]{1,0:T(8,128)S(1)} broadcast(f32[8]{0:T(128)} %param.16), dimensions={0} | broadcast | bytes 2080 | tf_op jit(solution)/shard_map/broadcast_in_dim | solution.py:411
  1.4 0.1 broadcast_in_dim_reshape.3.skip_ref
  1.5 2.6 %constant_dynamic-slice_fusion = (bf16[512,1,256]{2,1,0:T(2,128)(2,1)S(1)}, bf16[512,1,256]{2,1,0:T(2,128)(2,1)S(1)}) fusion(bf16[512,4,256]{2,1,0:T(4,128)(2,1)} %param.13, s32[]{:T(128)S(6)} %select_n.11, bf16[512,4,256]{2,1,0:T(4,128)(2,1)} %param.12), kind=kLoop, calls=%fused_computation.2 | loop fusion | bytes 1048580 | tf_op jit(solution)/shard_map/jit(dynamic_index_in_dim)/dynamic_slice | solution.py:366
  4.2 0.0 copy-start
  4.2 1.0 %copy-done = bf16[512,512]{1,0:T(8,128)(2,1)S(1)} copy-done((bf16[512,512]{1,0:T(8,128)(2,1)S(1)}, bf16[512,512]{1,0:T(8,128)(2,1)}, u32[]{:S(2)}) %copy-start) | copy-done | bytes 524312
  5.2 0.0 copy-start.1
  5.2 1.0 %copy-done.1 = bf16[512,512]{1,0:T(8,128)(2,1)S(1)} copy-done((bf16[512,512]{1,0:T(8,128)(2,1)S(1)}, bf16[512,512]{1,0:T(8,128)(2,1)}, u32[]{:S(2)}) %copy-start.1) | copy-done | bytes 524312
  6.3 0.0 copy-start.2
  6.3 1.0 %copy-done.2 = f32[8,64,256]{2,1,0:T(8,128)S(1)} copy-done((f32[8,64,256]{2,1,0:T(8,128)S(1)}, f32[8,64,256]{2,1,0:T(8,128)}, u32[]{:S(2)}) %copy-start.2) | copy-done | bytes 524312
  7.3 0.0 copy-start.3
  7.3 0.7 %copy-done.3 = f32[8,512]{1,0:T(8,128)S(1)} copy-done((f32[8,512]{1,0:T(8,128)S(1)}, f32[8,512]{1,0:T(8,128)}, u32[]{:S(2)}) %copy-start.3) | copy-done | bytes 16408
  8.0 0.0 copy-start.4
  8.0 0.7 %copy-done.4 = f32[8,512]{1,0:T(8,128)S(1)} copy-done((f32[8,512]{1,0:T(8,128)S(1)}, f32[8,512]{1,0:T(8,128)}, u32[]{:S(2)}) %copy-start.4) | copy-done | bytes 16408
  8.7 0.0 copy-start.5
  8.7 0.7 %copy-done.5 = f32[4,512]{1,0:T(4,128)S(1)} copy-done((f32[4,512]{1,0:T(4,128)S(1)}, f32[4,512]{1,0:T(4,128)}, u32[]{:S(2)}) %copy-start.5) | copy-done | bytes 8216
  9.4 53.0 %shard_map.121 = (bf16[512,512]{1,0:T(8,128)(2,1)S(1)}, bf16[512,512]{1,0:T(8,128)(2,1)S(1)}, f32[512,256]{1,0:T(8,128)S(1)}) custom-call(bf16[512,512]{1,0:T(8,128)(2,1)S(1)} %copy-done, bf16[512,512]{1,0:T(8,128)(2,1)S(1)} %copy-done.1, bf16[512,256]{1,0:T(8,128)(2,1)S(1)} %bitcast.9, bf16[512,256]{1,0:T(8,128)(2,1)S(1)} %bitcast.8, ...), custom_call_target="tpu_custom_call" | custom-call | tf_op jit(solution)/shard_map/pallas_call | solution.py:371
  62.4 0.8 %copy.24 = bf16[512,512]{1,0:T(8,128)(2,1)} copy(bf16[512,512]{1,0:T(8,128)(2,1)S(1)} %get-tuple-element.14) | data formatting | bytes 1048576
  63.2 0.8 %copy.25 = bf16[512,512]{1,0:T(8,128)(2,1)} copy(bf16[512,512]{1,0:T(8,128)(2,1)S(1)} %get-tuple-element.15) | data formatting | bytes 1048576
  64.0 0.8 %copy.26 = f32[1,8,64,256]{3,2,1,0:T(8,128)} copy(f32[1,8,64,256]{3,2,1,0:T(8,128)S(1)} %bitcast.11) | data formatting | bytes 1048576
  (2 shorter events, 0.1 us)
Async XLA Ops:
  4.2 1.0 %copy-start = (bf16[512,512]{1,0:T(8,128)(2,1)S(1)}, bf16[512,512]{1,0:T(8,128)(2,1)}, u32[]{:S(2)}) copy-start(bf16[512,512]{1,0:T(8,128)(2,1)} %grad_ref.1) | copy-start | bytes 1572868
  5.2 1.0 %copy-start.1 = (bf16[512,512]{1,0:T(8,128)(2,1)S(1)}, bf16[512,512]{1,0:T(8,128)(2,1)}, u32[]{:S(2)}) copy-start(bf16[512,512]{1,0:T(8,128)(2,1)} %conv_ref.1) | copy-start | bytes 1572868
  6.3 1.0 %copy-start.2 = (f32[8,64,256]{2,1,0:T(8,128)S(1)}, f32[8,64,256]{2,1,0:T(8,128)}, u32[]{:S(2)}) copy-start(f32[8,64,256]{2,1,0:T(8,128)} %param.18) | copy-start | bytes 1572868
  7.3 0.7 %copy-start.3 = (f32[8,512]{1,0:T(8,128)S(1)}, f32[8,512]{1,0:T(8,128)}, u32[]{:S(2)}) copy-start(f32[8,512]{1,0:T(8,128)} %step_ref.1) | copy-start | bytes 49156
  8.0 0.7 %copy-start.4 = (f32[8,512]{1,0:T(8,128)S(1)}, f32[8,512]{1,0:T(8,128)}, u32[]{:S(2)}) copy-start(f32[8,512]{1,0:T(8,128)} %decay_ref.1) | copy-start | bytes 49156
  8.7 0.7 %copy-start.5 = (f32[4,512]{1,0:T(4,128)S(1)}, f32[4,512]{1,0:T(4,128)}, u32[]{:S(2)}) copy-start(f32[4,512]{1,0:T(4,128)} %tap_ref.1) | copy-start | bytes 24580

commit v3 on v2

--- a/solution.py
+++ b/solution.py
@@ -10,29 +10,38 @@
 HD = 64
 HPG = 32
 KW = 4
-CHUNKS = 4
+PARTS = (3, 4, 4, 3, 2)
 REACH = 2
-FLYING = 2
+FLYING = 3
 RIM = 16
+VMEM_MIB = 60
 
 
 def layer_kernel(
     n_ctx,
     n_row,
     n_col,
+    grad_hbm,
+    conv_hbm,
+    step_hbm,
+    decay_hbm,
+    skip_hbm,
+    tap_hbm,
+    later_hbm,
+    w_hbm,
+    write_ref,
+    read_ref,
+    out_hbm,
+    x_hbm,
+    state_hbm,
+    out_ref,
+    state_ref,
     grad_ref,
     conv_ref,
-    write_ref,
-    read_ref,
     step_ref,
     decay_ref,
     skip_ref,
     tap_ref,
-    later_ref,
-    w_hbm,
-    out_ref,
-    x_ref,
-    state_ref,
     w_ref,
     pre_ref,
     carried_ref,
@@ -44,7 +53,8 @@
     staged,
     landed,
     own,
-    w_sem,
+    load_sem,
+    store_sem,
     col_send,
     col_recv,
     fwd_send,
@@ -56,12 +66,47 @@
     ctx = lax.axis_index("ctx")
     row = lax.axis_index("row")
     col = lax.axis_index("col")
-    step = gathered.shape[2]
-    width = gathered.shape[3]
+    tokens, width = grad_ref.shape
     d_out = out_ref.shape[1]
     mesh_id = pl.DeviceIdType.MESH
-
-    load_w = pltpu.make_async_copy(w_hbm, w_ref, w_sem)
+    has_next, has_previous = ctx < n_ctx - 1, ctx > 0
+
+    sizes = [tokens // sum(PARTS) * part for part in PARTS]
+    starts = [tokens - sum(sizes[: at + 1]) for at in range(len(PARTS))]
+    spans = [pl.ds(start, size) for start, size in zip(starts, sizes)]
+    chunks = range(len(PARTS))
+
+    pairs_of_refs = (
+        (decay_hbm, decay_ref),
+        (grad_hbm, grad_ref),
+        (step_hbm, step_ref),
+        (skip_hbm, skip_ref),
+        (tap_hbm, tap_ref),
+        (conv_hbm, conv_ref),
+        (w_hbm, w_ref),
+    )
+    loads = [
+        pltpu.make_async_copy(source, target, load_sem.at[at])
+        for at, (source, target) in enumerate(pairs_of_refs)
+    ]
+    load_decay, load_grad, load_step, load_skip, load_tap, load_conv, load_w = loads
+    load_later = pltpu.make_async_copy(later_hbm, carried_ref, load_sem.at[len(loads)])
+    for load in loads[:-1]:
+        load.start()
+    store_out = [
+        pltpu.make_async_copy(out_ref.at[span], out_hbm.at[span], store_sem.at[0, at])
+        for at, span in enumerate(spans)
+    ]
+    store_x = [
+        pltpu.make_async_copy(gathered.at[col, span], x_hbm.at[span], store_sem.at[1, at])
+        for at, span in enumerate(spans)
+    ]
+    store_state = pltpu.make_async_copy(state_ref, state_hbm, store_sem.at[2, 0])
+
+    @pl.when(jnp.logical_not(has_next))
+    def _():
+        load_later.start()
+
     load_w.start()
 
     barrier = pltpu.get_barrier_semaphore()
@@ -73,7 +118,6 @@
         pl.semaphore_signal(
             barrier, inc=1, device_id={"col": lax.rem(col + j, n_col)}, device_id_type=mesh_id
         )
-    has_next, has_previous = ctx < n_ctx - 1, ctx > 0
     for there, delta in ((has_next, 1), (has_previous, -1)):
 
         @pl.when(there)
@@ -86,8 +130,8 @@
 
     def col_copy(chunk, owner, target, sem):
         return pltpu.make_async_remote_copy(
-            src_ref=gathered.at[chunk, owner],
-            dst_ref=gathered.at[chunk, owner],
+            src_ref=gathered.at[owner, spans[chunk]],
+            dst_ref=gathered.at[owner, spans[chunk]],
             send_sem=sem,
             recv_sem=col_recv.at[chunk, owner],
             device_id={"col": target},
@@ -125,8 +169,8 @@
 
     def row_copy(chunk, target):
         return pltpu.make_async_remote_copy(
-            src_ref=staged.at[chunk, target],
-            dst_ref=landed.at[chunk, row],
+            src_ref=staged.at[target, spans[chunk]],
+            dst_ref=landed.at[row, spans[chunk]],
             send_sem=row_send.at[chunk, target],
             recv_sem=row_recv.at[chunk, row],
             device_id={"row": target},
@@ -134,27 +178,27 @@
         )
 
     def finish(chunk):
-        total = own[chunk]
+        total = own[spans[chunk]]
         for j in range(1, n_row):
             source = lax.rem(row + j, n_row)
             pltpu.make_async_remote_copy(
-                src_ref=staged.at[chunk, source],
-                dst_ref=landed.at[chunk, source],
+                src_ref=staged.at[source, spans[chunk]],
+                dst_ref=landed.at[source, spans[chunk]],
                 send_sem=row_send.at[chunk, source],
                 recv_sem=row_recv.at[chunk, source],
                 device_id={"row": source},
                 device_id_type=mesh_id,
             ).wait_recv()
-            total = total + landed[chunk, source].astype(jnp.float32)
-        first = pl.multiple_of((CHUNKS - 1 - chunk) * step, step)
-        out_ref[pl.ds(first, step), :] = total.astype(out_ref.dtype)
+            total = total + landed[source, spans[chunk]].astype(jnp.float32)
+        out_ref[spans[chunk], :] = total.astype(out_ref.dtype)
+        store_out[chunk].start()
 
     def product(chunk, target):
         rows = pl.ds(pl.multiple_of(target * d_out, d_out), d_out)
         total = None
         for owner in range(n_col):
             part = lax.dot_general(
-                gathered[chunk, owner],
+                gathered[owner, spans[chunk]],
                 w_ref[rows, owner * width : (owner + 1) * width],
                 (((1,), (1,)), ((), ())),
                 preferred_element_type=jnp.float32,
@@ -175,7 +219,6 @@
     pass_state = ctx_copy(0, state_out, state_in)
     pass_rim = ctx_copy(1, rim_out, rim_in)
 
-    tokens = grad_ref.shape[0]
     heads = decay_ref.shape[0]
     pairs = heads // 2
     lanes = 2 * HD
@@ -186,6 +229,7 @@
             a, b, (((a_dim,), (b_dim,)), ((), ())), preferred_element_type=f32
         )
 
+    load_decay.wait()
     decay = decay_ref[...]
     high = decay.astype(bf16)
     rest = decay - high.astype(f32)
@@ -199,7 +243,6 @@
         dot(high, triangle, 1, 0) + dot(middle, triangle, 1, 0) + dot(low, triangle, 1, 0)
     )
     by_token = cumulative.T
-    steps = step_ref[...].T
     grown = jnp.exp(by_token)
     left = jnp.exp(by_token[tokens - 1 : tokens, :] - by_token)
 
@@ -209,6 +252,7 @@
             lane < HD, columns[:, 2 * pair : 2 * pair + 1], columns[:, 2 * pair + 1 : 2 * pair + 2]
         )
 
+    load_grad.wait()
     weighted = jnp.concatenate(
         [
             (
@@ -231,7 +275,7 @@
 
     @pl.when(jnp.logical_not(has_next))
     def _():
-        carried_ref[...] = later_ref[...]
+        load_later.wait()
 
     for head in range(heads):
         rows = slice(head * HD, (head + 1) * HD)
@@ -244,7 +288,12 @@
     def _():
         pass_state.start()
 
+    store_state.start()
     carried = carried_ref[...].astype(bf16)
+    for load in (load_step, load_skip, load_tap, load_conv):
+        load.wait()
+    steps = step_ref[...].T
+    skips = skip_ref[...]
 
     def pre_rows(start, count):
         rows = slice(start, start + count)
@@ -269,7 +318,7 @@
             summed = intra + inter[:, columns] * spread(left[rows], pair, count)
             value = (
                 spread(steps[rows], pair, count) * summed
-                + skip_ref[:, columns] * grad_ref[rows, columns].astype(f32)
+                + spread(skips, pair, 1) * grad_ref[rows, columns].astype(f32)
             )
             v = conv_ref[rows, columns].astype(f32)
             q = 1.0 / (1.0 + jnp.exp(-v))
@@ -281,8 +330,8 @@
         rim_out[...] = pre_rows(0, RIM)
         pass_rim.start()
 
-    for chunk in range(CHUNKS):
-        start = tokens - (chunk + 1) * step
+    for chunk in chunks:
+        start, step = starts[chunk], sizes[chunk]
         pre_ref[start : start + step, :] = pre_rows(start, step).astype(f32)
         if chunk == 0:
 
@@ -299,49 +348,50 @@
         for tap in range(1, KW):
             mixed = mixed + tap_ref[tap : tap + 1, :] * pre_ref[start + tap : start + tap + step, :]
         mixed = mixed.astype(bf16)
-        x_ref[start : start + step, :] = mixed
-        gathered[chunk, col] = mixed
+        gathered[col, spans[chunk]] = mixed
+        store_x[chunk].start()
         if chunk < FLYING:
             send_chunk(chunk)
     load_w.wait()
 
-    def turn(chunk, carry):
+    for chunk in chunks:
         each_arrival(chunk, True, lambda copy: copy.start())
         each_send(chunk, lambda copy: copy.wait_send())
-
-        @pl.when(chunk + FLYING < CHUNKS)
-        def _():
+        if chunk + FLYING < len(PARTS):
             send_chunk(chunk + FLYING)
 
         @pl.loop(1, n_row)
         def _(j):
             target = lax.rem(row + j, n_row)
-            staged[chunk, target] = product(chunk, target).astype(jnp.bfloat16)
+            staged[target, spans[chunk]] = product(chunk, target).astype(bf16)
             row_copy(chunk, target).start()
 
-        own[chunk] = product(chunk, row)
-
-        @pl.when(chunk > 0)
-        def _():
+        own[spans[chunk]] = product(chunk, row)
+        if chunk > 0:
             finish(chunk - 1)
 
-        return carry
-
-    lax.fori_loop(0, CHUNKS, turn, 0)
-    finish(CHUNKS - 1)
-
-    def drain(chunk, carry):
+    finish(len(PARTS) - 1)
+    for chunk in chunks:
         each_arrival(chunk, False, lambda copy: copy.wait_send())
         for j in range(1, n_row):
             row_copy(chunk, lax.rem(row + j, n_row)).wait_send()
-        return carry
-
-    lax.fori_loop(0, CHUNKS, drain, 0)
 
     @pl.when(has_previous)
     def _():
         pass_state.wait_send()
         pass_rim.wait_send()
+
+    for store in (*store_out, *store_x, store_state):
+        store.wait()
+
+
+def hand_over(*refs):
+    sems = refs[6]
+    copies = [pltpu.make_async_copy(refs[at], refs[3 + at], sems.at[at]) for at in range(3)]
+    for copy in copies:
+        copy.start()
+    for copy in copies:
+        copy.wait()
 
 
 def on_device(
@@ -364,20 +414,34 @@
     group = head_block * heads // HPG
     write_rows = lax.dynamic_index_in_dim(input_mix, group, 1, keepdims=False)
     read_rows = lax.dynamic_index_in_dim(output_mix, group, 1, keepdims=False)
-    step = tokens // CHUNKS
     d_out = proj_weight.shape[0] // n_row
     in_vmem = pl.BlockSpec(memory_space=pltpu.VMEM)
+    anywhere = pl.BlockSpec(memory_space=pl.ANY)
     bf16, f32 = jnp.bfloat16, jnp.float32
-    hidden_grad, x_grad, state_grad = pl.pallas_call(
+    outputs = (
+        jax.ShapeDtypeStruct((tokens, d_out), bf16),
+        jax.ShapeDtypeStruct((tokens, width), bf16),
+        jax.ShapeDtypeStruct((width, states), f32),
+    )
+    loaded = (
+        output_grad,
+        conv_out,
+        step_size,
+        log_decay,
+        skip_gain.reshape(1, heads),
+        conv_weight,
+        later_grad.reshape(width, states),
+        proj_weight,
+    )
+    results = pl.pallas_call(
         functools.partial(layer_kernel, n_ctx, n_row, n_col),
-        out_shape=(
-            jax.ShapeDtypeStruct((tokens, d_out), bf16),
-            jax.ShapeDtypeStruct((tokens, width), bf16),
-            jax.ShapeDtypeStruct((width, states), f32),
-        ),
-        in_specs=[in_vmem] * 9 + [pl.BlockSpec(memory_space=pl.ANY)],
-        out_specs=(in_vmem,) * 3,
+        out_shape=outputs,
+        in_specs=[pl.BlockSpec(memory_space=pltpu.HBM)] * len(loaded) + [in_vmem] * 2,
+        out_specs=(anywhere,) * 3,
         scratch_shapes=[
+            pltpu.VMEM((tokens, d_out), bf16),
+            pltpu.VMEM((width, states), f32),
+            *(pltpu.VMEM(array.shape, array.dtype) for array in loaded[:6]),
             pltpu.VMEM(proj_weight.shape, bf16),
             pltpu.VMEM((tokens + RIM, width), f32),
             pltpu.VMEM((width, states), f32),
@@ -385,34 +449,32 @@
             pltpu.VMEM((width, states), bf16),
             pltpu.VMEM((RIM, width), bf16),
             pltpu.VMEM((RIM, width), bf16),
-            pltpu.VMEM((CHUNKS, n_col, step, width), bf16),
-            pltpu.VMEM((CHUNKS, n_row, step, d_out), bf16),
-            pltpu.VMEM((CHUNKS, n_row, step, d_out), bf16),
-            pltpu.VMEM((CHUNKS, step, d_out), f32),
-            pltpu.SemaphoreType.DMA,
-            pltpu.SemaphoreType.DMA((CHUNKS, 2 * REACH)),
-            pltpu.SemaphoreType.DMA((CHUNKS, n_col)),
-            pltpu.SemaphoreType.DMA((CHUNKS, 2, n_col)),
-            pltpu.SemaphoreType.DMA((CHUNKS, n_row)),
-            pltpu.SemaphoreType.DMA((CHUNKS, n_row)),
+            pltpu.VMEM((n_col, tokens, width), bf16),
+            pltpu.VMEM((n_row, tokens, d_out), bf16),
+            pltpu.VMEM((n_row, tokens, d_out), bf16),
+            pltpu.VMEM((tokens, d_out), f32),
+            pltpu.SemaphoreType.DMA((len(loaded),)),
+            pltpu.SemaphoreType.DMA((3, len(PARTS))),
+            pltpu.SemaphoreType.DMA((len(PARTS), 2 * REACH)),
+            pltpu.SemaphoreType.DMA((len(PARTS), n_col)),
+            pltpu.SemaphoreType.DMA((len(PARTS), 2, n_col)),
+            pltpu.SemaphoreType.DMA((len(PARTS), n_row)),
+            pltpu.SemaphoreType.DMA((len(PARTS), n_row)),
             pltpu.SemaphoreType.DMA((2,)),
             pltpu.SemaphoreType.DMA((2,)),
         ],
         compiler_params=pltpu.CompilerParams(
-            collective_id=0, has_side_effects=True, vmem_limit_bytes=48 << 20
+            collective_id=0, has_side_effects=True, vmem_limit_bytes=VMEM_MIB << 20
         ),
-    )(
-        output_grad,
-        conv_out,
-        write_rows,
-        read_rows,
-        step_size,
-        log_decay,
-        jnp.repeat(skip_gain, HD)[None, :],
-        conv_weight,
-        later_grad.reshape(width, states),
-        proj_weight,
-    )
+    )(*loaded, write_rows, read_rows)
+    hidden_grad, x_grad, state_grad = pl.pallas_call(
+        hand_over,
+        out_shape=outputs,
+        in_specs=[anywhere] * 3,
+        out_specs=(anywhere,) * 3,
+        scratch_shapes=[pltpu.SemaphoreType.DMA((3,))],
+        compiler_params=pltpu.CompilerParams(vmem_limit_bytes=VMEM_MIB << 20),
+    )(*results)
     return (hidden_grad, x_grad, state_grad.reshape(1, heads, HD, states))
 
 

time: 65.3 us -> 111 us (1.70)
  Pallas kernels: 53 us -> 106 us
  local copies, waits for them, and re-layouts: 11.1 us -> 4.11 us
    pallas_call x0 -> x1, Pallas kernels: none -> 48.8 us  [on_device(): pl.pallas_call(hand_over, out_shape=outputs, in_specs=[anywhere] * 3, out...]
    unnamed x17 -> x2, local copies, waits for them, and re-layouts: 7.71 us -> 1.48 us
    pallas_call x1, Pallas kernels: 53 us -> 57.5 us  [on_device(): pl.pallas_call(functools.partial(layer_kernel, n_ctx, n_row, n_col), out_...]
where the time goes in v3:
time: 111 us
  Pallas kernels  106 us (95%)
  local copies, waits for them, and re-layouts  4.11 us (4%)
    pallas_call x1, Pallas kernels, on_device(): pl.pallas_call(functools.partial(layer_kernel, n_ctx, n_row, n_col), out_...  57.5 us
    pallas_call x1, Pallas kernels, on_device(): pl.pallas_call(hand_over, out_shape=outputs, in_specs=[anywhere] * 3, out...  48.8 us
    dynamic_slice x1, local copies, waits for them, and re-layouts, on_device(): read_rows = lax.dynamic_index_in_dim(output_mix, group, 1, keepdims=False)  2.63 us

profile of v3, /device:TPU:0, one launch (start us, length us, event | category | flops | bytes accessed | tf_op | source)
XLA Modules:
  0.0 111.2 jit_solution(11639739690356677974)
XLA Ops:
  0.7 2.6 %constant_dynamic-slice_fusion = (bf16[512,1,256]{2,1,0:T(2,128)(2,1)S(1)}, bf16[512,1,256]{2,1,0:T(2,128)(2,1)S(1)}) fusion(bf16[512,4,256]{2,1,0:T(4,128)(2,1)} %param.13, s32[]{:T(128)S(6)} %select_n.11, bf16[512,4,256]{2,1,0:T(4,128)(2,1)} %param.12), kind=kLoop, calls=%fused_computation.2 | loop fusion | bytes 1048580 | tf_op jit(solution)/shard_map/jit(dynamic_index_in_dim)/dynamic_slice | solution.py:416
  3.3 0.7 copy.19
  4.0 0.7 copy.20
  4.8 57.5 %shard_map.121 = (bf16[512,512]{1,0:T(8,128)(2,1)}, bf16[512,512]{1,0:T(8,128)(2,1)}, f32[512,256]{1,0:T(8,128)}) custom-call(bf16[512,512]{1,0:T(8,128)(2,1)} %grad_hbm.1, bf16[512,512]{1,0:T(8,128)(2,1)} %conv_hbm.1, f32[8,512]{1,0:T(8,128)} %step_hbm.1, f32[8,512]{1,0:T(8,128)} %decay_hbm.1, f32[1,8]{1,0:T(1,128)} %bitcast.12, f32[4,512]{1,0:T(4,128)} %tap_hbm.1, ...), custom_call_target="tpu_custom_call" | custom-call | tf_op jit(solution)/shard_map/pallas_call | solution.py:436
  62.2 48.8 %shard_map.122 = (bf16[512,512]{1,0:T(8,128)(2,1)}, bf16[512,512]{1,0:T(8,128)(2,1)}, f32[512,256]{1,0:T(8,128)}) custom-call(bf16[512,512]{1,0:T(8,128)(2,1)} %get-tuple-element.9.refs_0_, bf16[512,512]{1,0:T(8,128)(2,1)} %get-tuple-element.10.refs_1_, f32[512,256]{1,0:T(8,128)} %get-tuple-element.11.refs_2_), custom_call_target="tpu_custom_call" | custom-call | tf_op jit(solution)/shard_map/pallas_call | solution.py:470

commit v4 on v3

--- a/solution.py
+++ b/solution.py
@@ -10,9 +10,9 @@
 HD = 64
 HPG = 32
 KW = 4
-PARTS = (3, 4, 4, 3, 2)
+PARTS = (4, 4, 3, 3, 2)
 REACH = 2
-FLYING = 3
+FLYING = 2
 RIM = 16
 VMEM_MIB = 60
 
@@ -386,12 +386,17 @@
 
 
 def hand_over(*refs):
-    sems = refs[6]
-    copies = [pltpu.make_async_copy(refs[at], refs[3 + at], sems.at[at]) for at in range(3)]
-    for copy in copies:
-        copy.start()
-    for copy in copies:
-        copy.wait()
+    count = len(refs) // 3
+    sources, targets, kept, sems = refs[:count], refs[count : 2 * count], refs[2 * count : -1], refs[-1]
+    takes = [pltpu.make_async_copy(sources[at], kept[at], sems.at[0, at]) for at in range(count)]
+    gives = [pltpu.make_async_copy(kept[at], targets[at], sems.at[1, at]) for at in range(count)]
+    for take in takes:
+        take.start()
+    for take, give in zip(takes, gives):
+        take.wait()
+        give.start()
+    for give in gives:
+        give.wait()
 
 
 def on_device(
@@ -472,7 +477,10 @@
         out_shape=outputs,
         in_specs=[anywhere] * 3,
         out_specs=(anywhere,) * 3,
-        scratch_shapes=[pltpu.SemaphoreType.DMA((3,))],
+        scratch_shapes=[
+            *(pltpu.VMEM(output.shape, output.dtype) for output in outputs),
+            pltpu.SemaphoreType.DMA((2, len(outputs))),
+        ],
         compiler_params=pltpu.CompilerParams(vmem_limit_bytes=VMEM_MIB << 20),
     )(*results)
     return (hidden_grad, x_grad, state_grad.reshape(1, heads, HD, states))

time: 111 us -> 64.4 us (0.58)
  Pallas kernels: 106 us -> 59.3 us
    pallas_call x1, Pallas kernels: 48.8 us -> 2.23 us  [on_device(): pl.pallas_call(hand_over, out_shape=outputs, in_specs=[anywhere] * 3, out...]
where the time goes in v4:
time: 64.4 us; the launch traced here: 64.2 us
  Pallas kernels  59.3 us (92%)
  local copies, waits for them, and re-layouts  4.11 us (6%)
  between operations  0.82 us (1%)
    pallas_call x1, Pallas kernels, on_device(): pl.pallas_call(functools.partial(layer_kernel, n_ctx, n_row, n_col), out_...  57 us
    dynamic_slice x1, local copies, waits for them, and re-layouts, on_device(): read_rows = lax.dynamic_index_in_dim(output_mix, group, 1, keepdims=False)  2.63 us
    pallas_call x1, Pallas kernels, on_device(): pl.pallas_call(hand_over, out_shape=outputs, in_specs=[anywhere] * 3, out...  2.23 us
    unnamed x2, local copies, waits for them, and re-layouts  1.48 us

profile of v4, /device:TPU:0, one launch (start us, length us, event | category | flops | bytes accessed | tf_op | source)
XLA Modules:
  0.0 64.2 jit_solution(1023272477874477179)
XLA Ops:
  0.7 2.6 %constant_dynamic-slice_fusion = (bf16[512,1,256]{2,1,0:T(2,128)(2,1)S(1)}, bf16[512,1,256]{2,1,0:T(2,128)(2,1)S(1)}) fusion(bf16[512,4,256]{2,1,0:T(4,128)(2,1)} %param.13, s32[]{:T(128)S(6)} %select_n.11, bf16[512,4,256]{2,1,0:T(4,128)(2,1)} %param.12), kind=kLoop, calls=%fused_computation.2 | loop fusion | bytes 1048580 | tf_op jit(solution)/shard_map/jit(dynamic_index_in_dim)/dynamic_slice | solution.py:421
  3.3 0.7 %copy.19 = bf16[512,1,256]{2,0,1:T(8,128)(2,1)} copy(bf16[512,1,256]{2,1,0:T(2,128)(2,1)S(1)} %get-tuple-element.15) | data formatting | bytes 524288
  4.0 0.7 %copy.20 = bf16[512,1,256]{2,0,1:T(8,128)(2,1)} copy(bf16[512,1,256]{2,1,0:T(2,128)(2,1)S(1)} %get-tuple-element.16) | data formatting | bytes 524288
  4.8 57.0 %shard_map.121 = (bf16[512,512]{1,0:T(8,128)(2,1)}, bf16[512,512]{1,0:T(8,128)(2,1)}, f32[512,256]{1,0:T(8,128)}) custom-call(bf16[512,512]{1,0:T(8,128)(2,1)} %grad_hbm.1, bf16[512,512]{1,0:T(8,128)(2,1)} %conv_hbm.1, f32[8,512]{1,0:T(8,128)} %step_hbm.1, f32[8,512]{1,0:T(8,128)} %decay_hbm.1, f32[1,8]{1,0:T(1,128)} %bitcast.12, f32[4,512]{1,0:T(4,128)} %tap_hbm.1, ...), custom_call_target="tpu_custom_call" | custom-call | tf_op jit(solution)/shard_map/pallas_call | solution.py:441
  61.8 2.2 %shard_map.122 = (bf16[512,512]{1,0:T(8,128)(2,1)}, bf16[512,512]{1,0:T(8,128)(2,1)}, f32[512,256]{1,0:T(8,128)}) custom-call(bf16[512,512]{1,0:T(8,128)(2,1)} %get-tuple-element.9.refs_0_, bf16[512,512]{1,0:T(8,128)(2,1)} %get-tuple-element.10.refs_1_, f32[512,256]{1,0:T(8,128)} %get-tuple-element.11.refs_2_), custom_call_target="tpu_custom_call" | custom-call | tf_op jit(solution)/shard_map/pallas_call | solution.py:475
